TPU v7x, 32 devices: a whole 2x2x4 slice. The times are simulated.
32 devices in a mesh: dp: 16 (over z, y, x), grp: 2 (over core).
Axes of the slice: x: 2, y: 2, z: 4, core: 2. Of those that a mesh axis runs over, the one named last changes fastest.
Arguments:
- audio: bfloat16 [384, 232, 320], P(('dp', 'grp')), may hold values from -3 to 3
- lengths: int32 [384], P('dp'), may hold values from 37 to 225, as said below
- codes: int32 [2, 2, 384, 232], P(None, None, 'dp'), may hold values from 0 to 1023
- disc_weight: bfloat16 [960, 512], replicated, may hold values from -0.1875 to 0.1875
- disc_score: float32 [512], replicated, may hold values from -0.25 to 0.25
- params: float32 [1441792], P('dp')
- params_mom: float32 [1441792], P('dp'), may hold values from -0.0009765625 to 0.0009765625
- params_avg: float32 [1441792], P('dp')
- books: float32 [2, 524288], P('grp', 'dp'), may hold values from -4 to 4
- books_mom: float32 [2, 524288], P('grp', 'dp'), may hold values from -3.8146973e-05 to 3.8146973e-05
- books_avg: float32 [2, 524288], P('grp', 'dp'), may hold values from -4 to 4
Outputs:
- params_new: float32 [1441792], P('dp')
- params_mom_new: float32 [1441792], P('dp')
- params_avg_new: float32 [1441792], P('dp')
- books_new: float32 [2, 524288], P('grp', 'dp')
- books_mom_new: float32 [2, 524288], P('grp', 'dp')
- books_avg_new: float32 [2, 524288], P('grp', 'dp')
- loss_sum: float32 [], replicated
- frame_count: float32 [], replicated
Inputs may be any that keep to these rules, and one draw needn't show every extreme that they name: lengths of the clips; 225 is reached in every draw.
All inputs are finite; a program needn't handle non-finite values.
Results may differ from a plain program's by a relative error of at most 0.0024.
Values may be sent and summed in bfloat16 or wider, within the bound.
A program may use at most 192 MiB of HBM per device.

v0:
```python
import functools
import math

import jax
import jax.numpy as jnp
import numpy as np
from jax import lax
from jax.experimental import pallas as pl
from jax.experimental.pallas import tpu as pltpu
from jax.sharding import PartitionSpec as P

BF = jnp.bfloat16
F32 = jnp.float32
MOMENTUM = 0.9
AVERAGE = 0.99
LANES = 256
CB = 1024
WIDE = 512
VMEM_LIMIT = 56 << 20


def spectral_table(samples):
    spots = np.arange(samples)[:, None]
    bins = np.arange(samples // 2)[None, :]
    turns = (spots * bins % samples) * (2.0 * math.pi / samples)
    window = 0.5 - 0.5 * np.cos((spots + 0.5) * (2.0 * math.pi / samples))
    table = np.concatenate([window * np.cos(turns), window * np.sin(turns)], axis=1)
    return (table * math.sqrt(2.0 / samples)).astype(np.float32)


def dot(left, right):
    return jnp.dot(left, right, preferred_element_type=F32)


def dot_nt(left, right):
    return lax.dot_general(left, right, (((1,), (1,)), ((), ())), preferred_element_type=F32)


def lanes(index, width):
    return pl.ds(pl.multiple_of(index * width, width), width)


def loop(bounds, step, hooks):
    hooks = dict(hooks)

    def body(index, carry):
        step(index)
        for after_index, hook in hooks.items():
            pl.when(index == after_index)(hook)
        return carry

    lax.fori_loop(*bounds, body, 0)


def col_sum(values):
    return jnp.sum(values, axis=0, keepdims=True)


def before(values):
    return pltpu.roll(values, 1, 1)


def after(values):
    return pltpu.roll(values, values.shape[1] - 1, 1)


def stack_three(values):
    return jnp.concatenate([before(values), values, after(values)], axis=0)


def silu_parts(values):
    sigmoid = 0.5 * jnp.tanh(0.5 * values) + 0.5
    return values * sigmoid, sigmoid * (1.0 + values * (1.0 - sigmoid))


def silu(values):
    return values * (0.5 * jnp.tanh(0.5 * values) + 0.5)


def load_signal(
    clip_count, side, fetch, free, lens, codes, pad, ipad, crow, mask, sig, hooks=()
):
    slots = codes.shape[3]
    pad[...] = jnp.zeros_like(pad)
    ipad[...] = jnp.full(ipad.shape, -1, jnp.int32)
    spots = lax.broadcasted_iota(jnp.int32, (1, LANES), 1)

    def step(clip):
        here = lanes(clip, LANES)
        row = side * clip_count + clip
        own = (spots < lens[row]).astype(F32)
        mask[:, here] = own
        for which in range(4):
            ipad[which : which + 1, 0:slots] = codes[which // 2, which % 2, pl.ds(row, 1), :]
        crow[:, here] = ipad[...]
        pad[:, 0:slots] = fetch(clip)[...]
        free(clip)
        wave = pad[...].astype(F32) * own
        sig[:, here] = wave.astype(BF)

    loop((0, clip_count), step, hooks)


def real_side(pairs, sig, disc_t, spec_t, feat_real, mag_real, hooks=()):
    samples = spec_t.shape[0]
    half = samples // 2

    def step(pair):
        here = lanes(pair, WIDE)
        wave = sig[:, here]
        feat_real[:, here] = silu(dot(disc_t[...], stack_three(wave))).astype(BF)
        spec = dot(spec_t[...], wave)
        norm = spec[:half] * spec[:half] + spec[half:] * spec[half:] + 1.0
        mag_real[:, here] = jnp.sqrt(norm)

    loop(pairs, step, hooks)


def onehot(crow, which, here, count):
    entries = lax.broadcasted_iota(jnp.int32, (CB, count), 0)
    return (entries == crow[pl.ds(which, 1), here]).astype(F32).astype(BF)


def encode(pairs, enc_t, sig, latent, hooks=()):
    def step(pair):
        here = lanes(pair, WIDE)
        latent[:, here] = dot(enc_t[...], stack_three(sig[:, here])).astype(BF)

    loop(pairs, step, hooks)


def pick(pairs, crow, mask, books_t, quant, slope, loss, hooks=()):
    half = books_t.shape[1]
    width = 2 * half

    def step(pair):
        here = lanes(pair, WIDE)
        own = mask[:, here]
        lost = jnp.zeros_like(own)
        for group in range(2):
            rows = slice(group * half, (group + 1) * half)
            hot = jnp.concatenate(
                [onehot(crow, 2 * group, here, WIDE), onehot(crow, 2 * group + 1, here, WIDE)], 0
            )
            value = dot(books_t[group], hot)
            quant[rows, here] = (value * own).astype(BF)
            gap = (slope[rows, here].astype(F32) - value) * own
            lost += col_sum(gap * gap)
            slope[rows, here] = (gap * (-2.0 / width)).astype(BF)
        loss[...] += lost * (1.0 / width)

    loop(pairs, step, hooks)


def book_grad(clip_count, crow, slope, which, rows):
    total = None
    chunk = 4 * LANES
    for part in range(clip_count * LANES // chunk):
        here = pl.ds(part * chunk, chunk)
        term = dot_nt(onehot(crow, which, here, chunk), slope[rows, here])
        total = term if total is None else total + term
    return total


def decode(pairs, refs, loss, hooks=()):
    (quant, dec_t, out, out_t, mask, sig, spec, spec_t, disc, disc_t, score_col) = refs[:11]
    (feat_real, mag_real, hidden, d_out, d_dec) = refs[11:]
    samples = spec.shape[0]
    width = hidden.shape[0]
    half = samples // 2

    def step(pair):
        here = lanes(pair, WIDE)
        own = mask[:, here]
        pre_dec = dot(dec_t[...], stack_three(quant[:, here]))
        act, act_slope = silu_parts(pre_dec)
        act = act.astype(BF)
        hidden[:, here] = act
        tanh_out = jnp.tanh(dot(out_t[...], act))
        made = tanh_out * own
        wave_gap = made - sig[:, here].astype(F32)
        norm = wave_gap * wave_gap + 1.0
        root = lax.rsqrt(norm)
        lost = col_sum(norm * root - 1.0) * (1.0 / samples)
        d_made = wave_gap * root * (1.0 / samples)
        made_low = made.astype(BF)

        spec_fake = dot(spec_t[...], made_low)
        real_part, imag_part = spec_fake[:half], spec_fake[half:]
        norm = real_part * real_part + imag_part * imag_part + 1.0
        root = lax.rsqrt(norm)
        spec_gap = norm * root - mag_real[:, here]
        norm = spec_gap * spec_gap + 1.0
        gap_root = lax.rsqrt(norm)
        lost += col_sum(norm * gap_root - 1.0) * (1.0 / samples)
        d_mag = spec_gap * gap_root * root * (1.0 / samples)
        d_spec = jnp.concatenate([d_mag * real_part, d_mag * imag_part], axis=0).astype(BF)
        d_made += dot(spec[...], d_spec)

        pre_fake = dot(disc_t[...], stack_three(made_low))
        feat_fake, feat_slope = silu_parts(pre_fake)
        weight = jnp.concatenate([score_col[...]] * (WIDE // 128), axis=1)
        miss = 1.0 - col_sum(feat_fake * weight)
        feat_gap = feat_fake - feat_real[:, here].astype(F32)
        norm = feat_gap * feat_gap + 1.0
        root = lax.rsqrt(norm)
        lost += own * (miss * miss + col_sum(norm * root - 1.0) * (1.0 / width))
        d_feat = (-2.0 * own * miss) * weight + (own * (1.0 / width)) * (feat_gap * root)
        d_fake = (d_feat * feat_slope).astype(BF)
        back = dot(disc[...], d_fake)
        d_made += after(back[:samples]) + back[samples : 2 * samples] + before(back[2 * samples :])

        d_pre_out = (d_made * own * (1.0 - tanh_out * tanh_out)).astype(BF)
        d_out[:, here] = d_pre_out
        d_dec[:, here] = (dot(out[...], d_pre_out) * act_slope).astype(BF)
        loss[...] += lost

    loop(pairs, step, hooks)


def latent_back(pairs, dec, d_dec, mask, slope, d_latent, hooks=()):
    width = d_dec.shape[0]

    def step(pair):
        here = lanes(pair, WIDE)
        back = dot(dec[...], d_dec[:, here])
        joined = after(back[:width]) + back[width : 2 * width] + before(back[2 * width :])
        joined = joined.astype(BF).astype(F32) * mask[:, here]
        d_latent[:, here] = (joined - slope[:, here].astype(F32)).astype(BF)

    loop(pairs, step, hooks)


def local_kernel(
    aud, lens, codes, disc, score, spec, spec_t, enc, dec, out, books,
    g_enc, g_dec, g_out, g_books, loss_out,
    pad, ipad, crow, mask, sig, disc_t, score_col, feat_real, mag_real,
    books_t, quant, hidden, enc_t, slope, dec_t, out_t, d_out, d_dec, loss,
):
    clip_count = aud.shape[0]
    pairs = (0, clip_count * LANES // WIDE)
    side = lax.axis_index("grp")
    loss[...] = jnp.zeros_like(loss)
    disc_t[...] = jnp.transpose(disc[...])
    score_col[...] = jnp.transpose(jnp.broadcast_to(score[...], (128, score.shape[1])))
    load_signal(
        clip_count, side, lambda clip: aud.at[clip], lambda clip: None, lens, codes, pad, ipad,
        crow, mask, sig,
    )
    real_side(pairs, sig, disc_t, spec_t, feat_real, mag_real)
    for group in range(2):
        books_t[group] = jnp.transpose(books[group])
    enc_t[...] = jnp.transpose(enc[...])
    dec_t[...] = jnp.transpose(dec[...])
    out_t[...] = jnp.transpose(out[...])
    encode(pairs, enc_t, sig, slope)
    pick(pairs, crow, mask, books_t, quant, slope, loss)

    def book_step(which, carry):
        rows = pl.ds(pl.multiple_of(which // 2 * 256, 256), 256)
        g_books[which] = book_grad(clip_count, crow, slope, which, rows)
        return carry

    lax.fori_loop(0, 4, book_step, 0)
    decode(
        pairs,
        (quant, dec_t, out, out_t, mask, sig, spec, spec_t, disc, disc_t, score_col,
         feat_real, mag_real, hidden, d_out, d_dec),
        loss,
    )
    g_out[...] = dot_nt(hidden[...], d_out[...])

    width = quant.shape[0]
    for part, shift in enumerate((before, lambda values: values, after)):
        g_dec[part * width : (part + 1) * width, :] = dot_nt(shift(quant[...]), d_dec[...])
    latent_back(pairs, dec, d_dec, mask, slope, hidden)

    samples = sig.shape[0]
    for part, shift in enumerate((before, lambda values: values, after)):
        g_enc[part * samples : (part + 1) * samples, :] = dot_nt(shift(sig[...]), hidden[...])
    loss_out[...] = loss[...]


def local_call(audio_t, lengths, codes, disc, score, enc, dec, out, books):
    clip_count, samples, _ = audio_t.shape
    width = disc.shape[1]
    total = clip_count * LANES
    table = spectral_table(samples)
    vmem = pl.BlockSpec(memory_space=pltpu.VMEM)
    smem = pl.BlockSpec(memory_space=pltpu.SMEM)
    return pl.pallas_call(
        local_kernel,
        out_shape=(
            jax.ShapeDtypeStruct((3 * samples, width), F32),
            jax.ShapeDtypeStruct((3 * width, width), F32),
            jax.ShapeDtypeStruct((width, samples), F32),
            jax.ShapeDtypeStruct((4, CB, width // 2), F32),
            jax.ShapeDtypeStruct((1, WIDE), F32),
        ),
        in_specs=[vmem, smem] + [vmem] * 9,
        out_specs=[vmem] * 5,
        scratch_shapes=[
            pltpu.VMEM((samples, LANES), BF),
            pltpu.VMEM((8, LANES), jnp.int32),
            pltpu.VMEM((8, total), jnp.int32),
            pltpu.VMEM((1, total), F32),
            pltpu.VMEM((samples, total), BF),
            pltpu.VMEM((width, 3 * samples), BF),
            pltpu.VMEM((width, 128), F32),
            pltpu.VMEM((width, total), BF),
            pltpu.VMEM((samples // 2, total), F32),
            pltpu.VMEM((2, width // 2, 2 * CB), BF),
            pltpu.VMEM((width, total), BF),
            pltpu.VMEM((width, total), BF),
            pltpu.VMEM((width, 3 * samples), BF),
            pltpu.VMEM((width, total), BF),
            pltpu.VMEM((width, 3 * width), BF),
            pltpu.VMEM((samples, width), BF),
            pltpu.VMEM((samples, total), BF),
            pltpu.VMEM((width, total), BF),
            pltpu.VMEM((1, WIDE), F32),
        ],
        compiler_params=pltpu.CompilerParams(vmem_limit_bytes=56 << 20),
        name="train_local",
    )(
        audio_t, lengths, codes, disc, score.reshape(1, width),
        jnp.asarray(table, BF), jnp.asarray(table.T, BF), enc, dec, out, books,
    )


def shards(
    audio, lengths, codes, disc_weight, disc_score, params, params_mom, params_avg, books,
    books_mom, books_avg,
):
    clip_count, slot_count, samples = audio.shape
    width = disc_weight.shape[1]
    half_width = width // 2
    side = lax.axis_index("grp")
    shared = lax.all_gather(params.astype(BF), "dp", axis=0, tiled=True)
    table = lax.all_gather(books.astype(BF), ("grp", "dp"), axis=1, tiled=True)
    enc_size = 3 * samples * width
    dec_size = 3 * width * width
    enc_weight = shared[:enc_size].reshape(3 * samples, width)
    dec_weight = shared[enc_size : enc_size + dec_size].reshape(3 * width, width)
    out_weight = shared[enc_size + dec_size :].reshape(width, samples)
    codebook = table.reshape(2, 2 * CB, half_width)
    local_count = jnp.sum(
        lax.dynamic_slice_in_dim(lengths, side * clip_count, clip_count, 0)
    ).astype(F32)
    frame_count = lax.psum(local_count, ("dp", "grp"))
    grad_enc, grad_dec, grad_out, grad_book, lost = local_call(
        jnp.swapaxes(audio, 1, 2), lengths, codes, disc_weight, disc_score,
        enc_weight, dec_weight, out_weight, codebook,
    )
    grad_shared = jnp.concatenate(
        [grad_enc.reshape(-1), grad_dec.reshape(-1), grad_out.reshape(-1)]
    )
    grad_shared = lax.psum(grad_shared.astype(BF), "grp").astype(F32)
    grad_book = lax.psum_scatter(
        grad_book.reshape(2, -1), "grp", scatter_dimension=0, tiled=True
    )
    shared_part = lax.psum_scatter(grad_shared, "dp", scatter_dimension=0, tiled=True)
    book_part = lax.psum_scatter(grad_book, "dp", scatter_dimension=1, tiled=True)
    loss_sum = lax.psum(jnp.sum(lost), ("dp", "grp"))
    all_clips = clip_count * lax.axis_size("dp") * lax.axis_size("grp")
    root = math.sqrt(131.0 * all_clips)
    shard_length = params.shape[0]
    spots = lax.axis_index("dp") * shard_length + jnp.arange(shard_length)
    rate = (
        jnp.where(spots < enc_size, 0.65, jnp.where(spots < enc_size + dec_size, 0.14, 0.2)) * root
    )
    shared_grad = shared_part / frame_count
    mom_new = MOMENTUM * params_mom + shared_grad
    param_new = params - rate * (shared_grad + MOMENTUM * mom_new)
    avg_new = AVERAGE * params_avg + (1.0 - AVERAGE) * param_new
    book_rate = 3.9 * math.sqrt(131.0 * all_clips * CB)
    book_grad_mean = book_part / frame_count
    book_mom_new = MOMENTUM * books_mom + book_grad_mean
    book_new = books - book_rate * (book_grad_mean + MOMENTUM * book_mom_new)
    book_avg_new = AVERAGE * books_avg + (1.0 - AVERAGE) * book_new
    return (
        param_new, mom_new, avg_new, book_new, book_mom_new, book_avg_new, loss_sum, frame_count,
    )


MESH = pl.DeviceIdType.MESH
ENC_RATE, DEC_RATE, OUT_RATE, BOOK_RATE = 0.65, 0.14, 0.2, 3.9
CHIPS = (4, 2, 2)
SENDS, ARRIVALS = 15, 71
WAVES = 4


def cols(index, width=128):
    return slice(index * width, (index + 1) * width)


def unflatten_out(flat, square):
    count = square.shape[1] // 2
    left = lax.broadcasted_iota(jnp.int32, (count, 128), 1) < 64
    part = [flat[pl.ds(k, count, stride=5), :] for k in range(5)]
    turned = [pltpu.roll(part[k], 64, 1) for k in (2, 3, 4)]
    even = part[:3]
    odd = [
        jnp.where(left, turned[0], turned[1]), jnp.where(left, turned[1], turned[2]), turned[2],
    ]
    for k in range(3):
        square[k, pl.ds(0, count, stride=2), :] = even[k]
        square[k, pl.ds(1, count, stride=2), :] = odd[k]


def flatten_out(square, flat):
    count = square.shape[1] // 2
    left = lax.broadcasted_iota(jnp.int32, (count, 128), 1) < 64
    even = [square[k, pl.ds(0, count, stride=2), :] for k in range(3)]
    odd = [square[k, pl.ds(1, count, stride=2), :] for k in range(3)]
    turned = [pltpu.roll(values, 64, 1) for values in odd]
    part = [
        even[0], even[1], jnp.where(left, even[2], turned[0]),
        jnp.where(left, turned[0], turned[1]), jnp.where(left, turned[1], turned[2]),
    ]
    for k in range(5):
        flat[pl.ds(k, count, stride=5), :] = part[k]


def update_kernel(
    all_clips, enc_chunks, dec_chunks, grad_p, grad_b, totals,
    par, pmom, pavg, bok, bmom, bavg,
    par_new, pmom_new, pavg_new, bok_new, bmom_new, bavg_new, loss, count,
):
    loss[0, 0] = totals[0, 0]
    count[0, 0] = totals[0, 1]
    frames = totals[0:1, 1:2]
    root = math.sqrt(131.0 * all_clips)
    where = lax.axis_index("dp") * par.shape[0] + lax.broadcasted_iota(jnp.int32, par.shape, 0)
    rate = root * jnp.where(
        where < enc_chunks, ENC_RATE,
        jnp.where(where < enc_chunks + dec_chunks, DEC_RATE, OUT_RATE),
    )

    def write(grad, rate, old, mom, avg, new_ref, mom_ref, avg_ref):
        grad = grad[...] / frames
        mom_new = MOMENTUM * mom[...] + grad
        new = old[...] - rate * (grad + MOMENTUM * mom_new)
        new_ref[...] = new
        mom_ref[...] = mom_new
        avg_ref[...] = AVERAGE * avg[...] + (1.0 - AVERAGE) * new

    write(grad_p, rate, par, pmom, pavg, par_new, pmom_new, pavg_new)
    write(grad_b, BOOK_RATE * root * math.sqrt(CB), bok, bmom, bavg, bok_new, bmom_new, bavg_new)


def fused_kernel(
    enc_rows, dec_rows,
    aud, lens, codes, disc, score, spec, spec_t, par, bok, grad_p, grad_b, totals,
    pad, ipad, crow, mask, sig, disc_t, score_col, feat_real, mag_real,
    books_t, quant, hidden, slope, dec_t, out, out_t, d_out, loss,
    weights, land, flat, square, acc_p, stage_p, got_p, acc_b,
    one_b, two_b, three_b, one_p, two_p, three_p,
    last, stat, zstat, waves, send, recv, wave_sem,
):
    clip_count = aud.shape[0]
    width, samples = disc_t.shape[0], sig.shape[0]
    half = width // 2
    pairs = clip_count * LANES // WIDE
    spot = lax.axis_index("dp")
    side = lax.axis_index("grp")
    other = 1 - side
    p_rows = par.shape[0] * 128 // width
    b_rows = bok.shape[0] * 128 // half
    out_rows = weights.shape[0] - enc_rows - dec_rows

    z, y, x = spot // 4, spot // 2 % 2, spot % 2
    mine_first = y + side * (x - y)
    mine_second = x + side * (y - x)

    def unit(level, first, second):
        return 4 * level + (2 - side) * first + (1 + side) * second

    def around(step):
        return (z + step) % 4

    first_dev = (unit(z, 1 - mine_first, mine_second), side)
    second_dev = (unit(z, mine_first, 1 - mine_second), side)
    pair_dev = (spot, other)

    def level_dev(level):
        return (unit(level, mine_first, mine_second), side)

    barrier = pltpu.get_barrier_semaphore()
    near = [first_dev, second_dev, pair_dev] + [level_dev(around(k)) for k in (1, 2, 3)]
    for device in near:
        pl.semaphore_signal(barrier, inc=1, device_id=device, device_id_type=MESH)

    def wave_copy(clip, slot):
        return pltpu.make_async_copy(aud.at[clip], waves.at[slot], wave_sem.at[slot])

    for slot in range(WAVES):
        wave_copy(slot, slot).start()
    taken = {"send": 0, "recv": 0}

    def take(kind, count=1):
        taken[kind] += count
        return taken[kind] - count

    def copy_to(device, src, dst, send_at, recv_at):
        return pltpu.make_async_remote_copy(
            src_ref=src, dst_ref=dst, send_sem=send.at[send_at], recv_sem=recv.at[recv_at],
            device_id=device, device_id_type=MESH,
        )

    def block(ref, rows, which):
        return ref.at[pl.ds(pl.multiple_of(which * rows, 16), rows), :]

    def p_view(which, count=1):
        rows = pl.ds(pl.multiple_of(which * p_rows, 16), count * p_rows)
        return weights.at[rows, lanes(side, half)]

    def b_view(which, count=1):
        rows = pl.ds(pl.multiple_of(which * b_rows, 16), count * b_rows)
        return land.at[side, rows, :]

    def held(span, which, run):
        if span is None:
            run()
        else:
            pl.when((which >= span[0]) & (which < span[1]))(run)

    def wait_sent(ref, at):
        copy_to(pair_dev, ref, ref, at, 0).wait_send()

    def wait_got(ref, at):
        copy_to(pair_dev, ref, ref, 0, at).wait_recv()

    class Slots:
        def __init__(self):
            self.sent = take("send")
            self.got = take("recv", 15)

    class Gather:
        def __init__(self, view, span, slots):
            self.view, self.span, self.slots = view, span, slots
            self.swap_sent, self.swap_got = take("send"), take("recv")

            def make(slot, which, device):
                return copy_to(
                    device, view(which), view(which), slots.sent, slots.got + slot
                )

            self.levels, self.firsts, self.seconds = [], [], []
            for k in range(4):
                here = unit(around(4 - k), mine_first, mine_second)
                there = unit(around(4 - k), 1 - mine_first, mine_second)
                if k:
                    self.levels.append(make(k - 1, spot, level_dev(around(k))))
                self.firsts.append(make(3 + k, here, first_dev))
                self.seconds.append(
                    [make(7 + 2 * k, here, second_dev), make(8 + 2 * k, there, second_dev)]
                )

        def swap(self, which):
            copy_to(
                pair_dev, self.view(which), self.view(which), self.swap_sent, self.swap_got
            ).start()

        def start(self):
            def run():
                for copy in self.levels + [self.firsts[0], self.seconds[0][0]]:
                    copy.start()
                self.swap(spot)

            held(self.span, spot, run)

        def step(self):
            for k in (1, 2, 3):
                which = unit(around(4 - k), mine_first, mine_second)

                def run(k=k, which=which):
                    self.levels[k - 1].wait_recv()
                    self.firsts[k].start()
                    self.seconds[k][0].start()
                    self.swap(which)

                held(self.span, which, run)

        def back(self, ks):
            for k in ks:
                which = unit(around(4 - k), 1 - mine_first, mine_second)

                def run(k=k, which=which):
                    self.firsts[k].wait_recv()
                    self.seconds[k][1].start()
                    self.swap(which)

                held(self.span, which, run)

        def finish(self, ks):
            for k in ks:
                for slot, first in enumerate((mine_first, 1 - mine_first)):
                    which = unit(around(4 - k), first, 1 - mine_second)

                    def run(k=k, slot=slot, which=which):
                        self.seconds[k][slot].wait_recv()
                        self.swap(which)

                    held(self.span, which, run)

        def settle(self):
            wait_got(self.view(*self.span_units()), self.swap_got)
            wait_sent(self.view(*self.span_units()), self.swap_sent)

        def span_units(self):
            start, stop = self.span or (0, 16)
            return start, stop - start

    class Scatter:
        def __init__(self, span, rows, acc, stage, got, landed, slots):
            self.span, self.rows, self.acc, self.stage, self.got = span, rows, acc, stage, got
            self.landed, self.slots = landed, slots
            start, stop = span or (0, 16)
            self.levels = list(range(start // 4, (stop + 3) // 4))
            both_rows = pl.ds(start * rows, (stop - start) * rows)
            self.pair = copy_to(
                pair_dev, stage.at[both_rows, :], got.at[both_rows, :], take("send"), take("recv")
            )
            one, two, three = landed
            self.sent_one, self.kept_one, self.sent_two, self.kept_two = [], [], [], []
            for level in self.levels:
                for first in range(2):
                    slot = 2 * level + first
                    which = unit(level, first, 1 - mine_second)
                    self.sent_one.append((which, copy_to(
                        second_dev, block(stage, rows, which), one.at[slot],
                        slots.sent, slots.got + slot,
                    )))
                    self.kept_one.append((unit(level, first, mine_second), one, slot))
                which = unit(level, 1 - mine_first, mine_second)
                self.sent_two.append((which, copy_to(
                    first_dev, block(stage, rows, which), two.at[level],
                    slots.sent, slots.got + 8 + level,
                )))
                self.kept_two.append((unit(level, mine_first, mine_second), two, level))

        def read(self, ref, which):
            return ref[pl.ds(pl.multiple_of(which * self.rows, 16), self.rows), :]

        def put(self, ref, which, values):
            ref[pl.ds(pl.multiple_of(which * self.rows, 16), self.rows), :] = values

        def round_one(self):
            self.pair.wait()
            for which, copy in self.sent_one:
                def run(which=which, copy=copy):
                    total = self.read(self.acc, which) + self.read(self.got, which).astype(F32)
                    self.put(self.stage, which, total.astype(BF))
                    copy.start()

                held(self.span, which, run)
            for which, _, _ in self.kept_one:
                def keep(which=which):
                    total = self.read(self.acc, which) + self.read(self.got, which).astype(F32)
                    self.put(self.acc, which, total)

                held(self.span, which, keep)

        def fold(self, kept, sent):
            for (which, landed, slot), (_, copy) in zip(kept, sent):
                def run(which=which, landed=landed, slot=slot, copy=copy):
                    copy.wait_recv()
                    self.put(
                        self.acc, which, self.read(self.acc, which) + landed[slot].astype(F32)
                    )

                held(self.span, which, run)

        def round_two(self):
            self.fold(self.kept_one, self.sent_one)
            for which, copy in self.sent_two:
                def run(which=which, copy=copy):
                    self.put(self.stage, which, self.read(self.acc, which).astype(BF))
                    copy.start()

                held(self.span, which, run)

        def round_three(self):
            self.fold(self.kept_two, self.sent_two)
            for level in self.levels:
                which = unit(level, mine_first, mine_second)
                slot = (z + 7 - level) % 4 % 3

                def run(level=level, which=which, slot=slot):
                    self.put(self.stage, which, self.read(self.acc, which).astype(BF))
                    copy_to(
                        level_dev(level), block(self.stage, self.rows, which),
                        self.landed[2].at[slot], self.slots.sent, self.slots.got + 12 + slot,
                    ).start()

                pl.when(z != level)(functools.partial(held, self.span, which, run))

        def settle(self):
            def run():
                total = self.read(self.acc, spot)
                for slot in range(3):
                    wait_got(self.landed[2].at[slot], self.slots.got + 12 + slot)
                    total = total + self.landed[2][slot].astype(F32)
                self.put(self.acc, spot, total)

            held(self.span, spot, run)

        def drain(self):
            wait_sent(self.stage.at[0 : 15 * self.rows, :], self.slots.sent)

    for j in range(2):
        spots = pl.ds(pl.multiple_of(side * half + j * 128, 128), 128)
        weights[pl.ds(pl.multiple_of(spot * p_rows, 16), p_rows), spots] = par[
            pl.ds(2 * side + j, p_rows, stride=4), :
        ].astype(BF)
        land[side, pl.ds(pl.multiple_of(spot * b_rows, 16), b_rows), cols(j)] = bok[
            pl.ds(j, b_rows, stride=2), :
        ].astype(BF)
    slots_b, slots_p = Slots(), Slots()
    gather_b = Gather(b_view, None, slots_b)
    gather_p, gather_q = Gather(p_view, (0, 6), slots_p), Gather(p_view, (6, 16), slots_p)
    pl.semaphore_wait(barrier, len(near))
    gather_p.start()
    gather_b.start()
    loss[...] = jnp.zeros_like(loss)
    disc_t[...] = jnp.transpose(disc[...])
    score_col[...] = jnp.transpose(jnp.broadcast_to(score[...], (128, score.shape[1])))

    def fetch(clip):
        wave_copy(clip, clip % WAVES).wait()
        return waves.at[clip % WAVES]

    def free(clip):
        @pl.when(clip + WAVES < clip_count)
        def _():
            wave_copy(clip + WAVES, clip % WAVES).start()

    def both(*steps):
        def run():
            for step in steps:
                step()

        return run

    part = functools.partial
    early, late, every = (0,), (1, 2, 3), (0, 1, 2, 3)
    load_signal(
        clip_count, side, fetch, free, lens, codes, pad, ipad, crow, mask, sig,
        {7: both(part(gather_p.back, early), part(gather_b.back, early))},
    )
    real_side(
        (0, pairs), sig, disc_t, spec_t, feat_real, mag_real,
        {2: gather_p.step, 4: gather_b.step, 5: part(gather_p.back, late)},
    )
    gather_p.finish(every)
    gather_b.back(late)
    gather_p.settle()
    enc = weights.at[0:enc_rows, :]
    dec = weights.at[enc_rows : enc_rows + dec_rows, :]
    enc_t = dec_t.at[:, 0:enc_rows]
    enc_t[...] = jnp.transpose(enc[...])
    encode(
        (0, pairs), enc_t, sig, slope,
        {0: gather_q.start, 2: part(gather_b.finish, every), 5: part(gather_q.back, early)},
    )
    gather_b.settle()
    for group in range(2):
        books_t[group] = jnp.transpose(land[group])
    wait_sent(b_view(0, 15), slots_b.sent)
    pick(
        (0, pairs), crow, mask, books_t, quant, slope, loss,
        {1: gather_q.step, 3: part(gather_q.back, late), 5: part(gather_q.finish, every)},
    )

    d_dec = feat_real
    stage_b, got_b = land.at[0], land.at[1]
    scatter_b = Scatter(None, b_rows, acc_b, stage_b, got_b, (one_b, two_b, three_b), Slots())

    def far_books(level, carry):
        rows = pl.ds(pl.multiple_of(other * half, half), half)
        values = book_grad(clip_count, crow, slope, 2 * other + level, rows)
        stage_b[lanes(level, CB), :] = values.astype(BF)
        return carry

    def near_books(level, carry):
        rows = pl.ds(pl.multiple_of(side * half, half), half)
        acc_b[lanes(level, CB), :] = book_grad(clip_count, crow, slope, 2 * side + level, rows)
        return carry

    lax.fori_loop(0, 2, far_books, 0)
    gather_q.settle()
    scatter_b.pair.start()
    lax.fori_loop(0, 2, near_books, 0)
    wait_sent(p_view(0, 15), slots_p.sent)
    scatter_b.round_one()

    dec_t[...] = jnp.transpose(dec[...])
    for j in range(4):
        flat[pl.ds(j, out_rows, stride=4), :] = weights[
            enc_rows + dec_rows :, cols(j)
        ].astype(F32)
    unflatten_out(flat, square)
    edges = [(k, k * 128, min(k * 128 + 128, samples)) for k in range(3)]
    for k, start, stop in edges:
        out[:, start:stop] = square[k, :, 0 : stop - start].astype(BF)
    out_t[...] = jnp.transpose(out[...])
    decode_refs = (
        quant, dec_t, out, out_t, mask, sig, spec, spec_t, disc, disc_t, score_col,
        feat_real, mag_real, hidden, d_out, d_dec,
    )
    decode(
        (0, pairs), decode_refs, loss, {1: scatter_b.round_two, 3: scatter_b.round_three}
    )

    grad_out = dot_nt(hidden[...], d_out[...])
    for k, start, stop in edges:
        square[k, :, 0 : stop - start] = grad_out[:, start:stop]
    flatten_out(square, flat)
    low = enc_rows + dec_rows
    for j in range(2):
        near_part = flat[pl.ds(2 * side + j, out_rows, stride=4), :]
        far_part = flat[pl.ds(2 * other + j, out_rows, stride=4), :]
        acc_p[low : low + out_rows, cols(j)] = near_part
        stage_p[low : low + out_rows, cols(j)] = far_part.astype(BF)

    landed, slots = (one_p, two_p, three_p), Slots()
    scatter_d = Scatter((6, 16), p_rows, acc_p, stage_p, got_p, landed, slots)
    scatter_e = Scatter((0, 6), p_rows, acc_p, stage_p, got_p, landed, slots)
    near_rows = pl.ds(pl.multiple_of(side * half, half), half)
    far_rows = pl.ds(pl.multiple_of(other * half, half), half)
    for k, shift in ((1, None), (0, before), (2, after)):
        values = quant
        if shift is not None:
            values = hidden
            hidden[...] = shift(quant[...])
        rows = slice(enc_rows + k * width, enc_rows + (k + 1) * width)
        stage_p[rows, :] = dot_nt(values[...], d_dec[far_rows, :]).astype(BF)
        if k == 2:
            scatter_d.pair.start()
            scatter_b.settle()
            scatter_b.drain()
        acc_p[rows, :] = dot_nt(values[...], d_dec[near_rows, :])
    d_out[...] = before(sig[...])
    hidden[0:samples, :] = after(sig[...])
    shifted = (d_out, sig, hidden.at[0:samples, :])
    valid = jnp.sum(mask[...])
    lost = jnp.sum(loss[...])
    first_lane = lax.broadcasted_iota(jnp.int32, (8, 128), 1) == 0
    stat[0] = jnp.where(first_lane, lost, valid)
    swaps = [
        copy_to(device, stat.at[2 * k], stat.at[2 * k + 1], take("send"), take("recv"))
        for k, device in enumerate((pair_dev, first_dev, second_dev))
    ]
    level_sent, level_got = take("send"), take("recv")
    swaps[0].start()

    def stat_two():
        swaps[0].wait()
        stat[2] = stat[0] + stat[1]
        swaps[1].start()

    def stat_three():
        swaps[1].wait()
        stat[4] = stat[2] + stat[3]
        swaps[2].start()

    latent_back(
        (0, pairs), dec, d_dec, mask, slope, slope,
        {
            0: scatter_d.round_one,
            1: stat_two,
            3: stat_three,
            5: scatter_d.round_two,
        },
    )
    swaps[2].wait()
    zstat[z] = stat[4] + stat[5]
    for k in (1, 2, 3):
        copy_to(level_dev(around(k)), zstat.at[z], zstat.at[z], level_sent, level_got).start()
    for k, values in enumerate(shifted):
        rows = slice(k * samples, (k + 1) * samples)
        stage_p[rows, :] = dot_nt(values[...], slope[far_rows, :]).astype(BF)
    scatter_e.pair.start()
    for k, values in enumerate(shifted):
        rows = slice(k * samples, (k + 1) * samples)
        acc_p[rows, :] = dot_nt(values[...], slope[near_rows, :])
    scatter_e.round_one()
    scatter_d.round_three()
    wait_got(zstat.at[0:3], level_got)
    wait_sent(zstat.at[0:3], level_sent)
    totals[...] = (zstat[0] + zstat[1]) + (zstat[2] + zstat[3])
    own_b = pl.ds(pl.multiple_of(spot * b_rows, 16), b_rows)
    for j in range(2):
        grad_b[pl.ds(j, b_rows, stride=2), :] = acc_b[own_b, cols(j)]
    scatter_e.round_two()
    scatter_d.settle()
    scatter_e.round_three()
    scatter_e.settle()

    own_p = pl.ds(pl.multiple_of(spot * p_rows, 16), p_rows)
    swap = copy_to(pair_dev, acc_p.at[own_p, :], last, take("send"), take("recv"))
    swap.start()
    for j in range(2):
        grad_p[pl.ds(2 * side + j, p_rows, stride=4), :] = acc_p[own_p, cols(j)]
    scatter_e.drain()
    swap.wait()
    for j in range(2):
        grad_p[pl.ds(2 * other + j, p_rows, stride=4), :] = last[:, cols(j)]
    assert taken == {"send": SENDS, "recv": ARRIVALS}, taken


def fused(
    audio, lengths, codes, disc_weight, disc_score, params, params_mom, params_avg, books,
    books_mom, books_avg,
):
    clip_count, _, samples = audio.shape
    width = disc_weight.shape[1]
    half = width // 2
    chips = lax.axis_size("dp")
    total = clip_count * LANES
    table = spectral_table(samples)
    p_rows, b_rows = params.shape[0] // width, books.shape[1] // half
    all_rows, book_rows = p_rows * chips, b_rows * chips
    vmem = pl.BlockSpec(memory_space=pltpu.VMEM)
    smem = pl.BlockSpec(memory_space=pltpu.SMEM)
    p_shape = (params.shape[0] // 128, 128)
    b_shape = (books.shape[1] // 128, 128)
    all_clips = clip_count * chips * lax.axis_size("grp")
    weights = [value.reshape(p_shape) for value in (params, params_mom, params_avg)]
    tables = [value.reshape(b_shape) for value in (books, books_mom, books_avg)]
    grad_shapes = [jax.ShapeDtypeStruct(p_shape, F32), jax.ShapeDtypeStruct(b_shape, F32)]
    grads = pl.pallas_call(
        functools.partial(fused_kernel, 3 * samples, 3 * width),
        out_shape=grad_shapes + [jax.ShapeDtypeStruct((8, 128), F32)],
        in_specs=[pl.BlockSpec(memory_space=pl.ANY), smem] + [vmem] * 7,
        out_specs=[vmem] * 3,
        scratch_shapes=[
            pltpu.VMEM((samples, LANES), BF),
            pltpu.VMEM((8, LANES), jnp.int32),
            pltpu.VMEM((8, total), jnp.int32),
            pltpu.VMEM((1, total), F32),
            pltpu.VMEM((samples, total), BF),
            pltpu.VMEM((width, 3 * samples), BF),
            pltpu.VMEM((width, 128), F32),
            pltpu.VMEM((width, total), BF),
            pltpu.VMEM((samples // 2, total), F32),
            pltpu.VMEM((2, half, 2 * CB), BF),
            pltpu.VMEM((width, total), BF),
            pltpu.VMEM((width, total), BF),
            pltpu.VMEM((width, total), BF),
            pltpu.VMEM((width, 3 * width), BF),
            pltpu.VMEM((width, samples), BF),
            pltpu.VMEM((samples, width), BF),
            pltpu.VMEM((samples, total), BF),
            pltpu.VMEM((1, WIDE), F32),
            pltpu.VMEM((all_rows, width), BF),
            pltpu.VMEM((2, book_rows, half), BF),
            pltpu.VMEM((width * samples // 128, 128), F32),
            pltpu.VMEM((3, width, 128), F32),
            pltpu.VMEM((all_rows, half), F32),
            pltpu.VMEM((all_rows, half), BF),
            pltpu.VMEM((all_rows, half), BF),
            pltpu.VMEM((book_rows, half), F32),
            pltpu.VMEM((8, b_rows, half), BF),
            pltpu.VMEM((4, b_rows, half), BF),
            pltpu.VMEM((3, b_rows, half), BF),
            pltpu.VMEM((8, p_rows, half), BF),
            pltpu.VMEM((4, p_rows, half), BF),
            pltpu.VMEM((3, p_rows, half), BF),
            pltpu.VMEM((p_rows, half), F32),
            pltpu.VMEM((6, 8, 128), F32),
            pltpu.VMEM((4, 8, 128), F32),
            pltpu.VMEM((WAVES, samples, audio.shape[1]), BF),
            pltpu.SemaphoreType.DMA((SENDS,)),
            pltpu.SemaphoreType.DMA((ARRIVALS,)),
            pltpu.SemaphoreType.DMA((WAVES,)),
        ],
        compiler_params=pltpu.CompilerParams(
            vmem_limit_bytes=VMEM_LIMIT, collective_id=0, has_side_effects=True
        ),
        name="train_step",
    )(
        jnp.swapaxes(audio, 1, 2), lengths, codes, disc_weight, disc_score.reshape(1, width),
        jnp.asarray(table, BF), jnp.asarray(table.T, BF), weights[0], tables[0],
    )
    outs = pl.pallas_call(
        functools.partial(
            update_kernel, all_clips, 3 * samples * width // 128, 3 * width * width // 128
        ),
        out_shape=[grad_shapes[0]] * 3 + [grad_shapes[1]] * 3
        + [jax.ShapeDtypeStruct((1, 1), F32)] * 2,
        in_specs=[vmem] * 9,
        out_specs=[vmem] * 6 + [smem] * 2,
        name="train_update",
    )(*grads, *weights, *tables)
    return (
        *(value.reshape(params.shape) for value in outs[:3]),
        *(value.reshape(books.shape) for value in outs[3:6]),
        outs[6].reshape(()),
        outs[7].reshape(()),
    )


def solution(mesh):
    in_specs = (
        P(("dp", "grp"), None, None), P("dp"), P(None, None, "dp", None), P(), P(), P("dp"),
        P("dp"), P("dp"), P("grp", "dp"), P("grp", "dp"), P("grp", "dp"),
    )
    out_specs = (
        P("dp"), P("dp"), P("dp"), P("grp", "dp"), P("grp", "dp"), P("grp", "dp"), P(), P(),
    )
    body = fused if mesh.shape["dp"] == math.prod(CHIPS) else shards
    return jax.shard_map(body, mesh=mesh, in_specs=in_specs, out_specs=out_specs, check_vma=False)
```

profile of v0, /device:TPU:0, one launch (start us, length us, event | category | flops | bytes accessed | tf_op | source)
XLA Modules:
  0.0 130.5 jit_solution(16273986759745802401)
XLA Ops:
  0.6 126.8 %train_step.1 = (f32[704,128]{1,0:T(8,128)}, f32[256,128]{1,0:T(8,128)}, f32[8,128]{1,0:T(8,128)}) custom-call(bf16[12,320,232]{2,1,0:T(8,128)(2,1)} %bitcast.16, s32[24]{0:T(128)} %lens.1, s32[2,2,24,232]{3,2,1,0:T(8,128)} %codes.1, bf16[960,512]{1,0:T(8,128)(2,1)} %disc.1, f32[1,512]{1,0:T(1,128)} %bitcast.25, bf16[320,320]{1,0:T(8,128)(2,1)} %constant.4.clone.spec, ...), custom_call_target="tpu_custom_call" | custom-call | tf_op jit(solution)/shard_map/train_step/pallas_call | solution.py:933
  127.5 2.8 %train_update.1 = (f32[704,128]{1,0:T(8,128)}, f32[704,128]{1,0:T(8,128)}, f32[704,128]{1,0:T(8,128)}, f32[256,128]{1,0:T(8,128)}, f32[256,128]{1,0:T(8,128)}, /...) custom-call(f32[704,128]{1,0:T(8,128)} %get-tuple-element.19.grad_p, f32[256,128]{1,0:T(8,128)} %get-tuple-element.20.grad_b, ...), custom_call_target="tpu_custom_call" | custom-call | tf_op jit(solution)/shard_map/train_update/pallas_call | solution.py:987
where the time goes:
time: 131 us; the launch traced here: 130 us
  Pallas kernels  130 us (99%)
    pallas_call x1, Pallas kernels, fused(): pl.pallas_call(functools.partial(fused_kernel, 3 * samples, 3 * width), o...  127 us
    pallas_call x1, Pallas kernels, fused(): pl.pallas_call(functools.partial(update_kernel, all_clips, 3 * samples *...  2.81 us

commit v1 on v0

--- a/solution.py
+++ b/solution.py
@@ -386,7 +386,7 @@
 MESH = pl.DeviceIdType.MESH
 ENC_RATE, DEC_RATE, OUT_RATE, BOOK_RATE = 0.65, 0.14, 0.2, 3.9
 CHIPS = (4, 2, 2)
-SENDS, ARRIVALS = 15, 71
+SENDS, ARRIVALS = 16, 72
 WAVES = 4
 
 
@@ -723,6 +723,7 @@
     pl.semaphore_wait(barrier, len(near))
     gather_p.start()
     gather_b.start()
+    gather_q.start()
     loss[...] = jnp.zeros_like(loss)
     disc_t[...] = jnp.transpose(disc[...])
     score_col[...] = jnp.transpose(jnp.broadcast_to(score[...], (128, score.shape[1])))
@@ -747,14 +748,15 @@
     early, late, every = (0,), (1, 2, 3), (0, 1, 2, 3)
     load_signal(
         clip_count, side, fetch, free, lens, codes, pad, ipad, crow, mask, sig,
-        {7: both(part(gather_p.back, early), part(gather_b.back, early))},
+        {7: both(part(gather_p.back, early), part(gather_b.back, early), part(gather_q.back, early))},
     )
     real_side(
         (0, pairs), sig, disc_t, spec_t, feat_real, mag_real,
-        {2: gather_p.step, 4: gather_b.step, 5: part(gather_p.back, late)},
-    )
+        {3: gather_p.step, 4: gather_b.step, 5: part(gather_p.back, late)},
+    )
+    gather_q.step()
+    gather_b.back(late)
     gather_p.finish(every)
-    gather_b.back(late)
     gather_p.settle()
     enc = weights.at[0:enc_rows, :]
     dec = weights.at[enc_rows : enc_rows + dec_rows, :]
@@ -762,7 +764,7 @@
     enc_t[...] = jnp.transpose(enc[...])
     encode(
         (0, pairs), enc_t, sig, slope,
-        {0: gather_q.start, 2: part(gather_b.finish, every), 5: part(gather_q.back, early)},
+        {0: part(gather_q.back, late), 2: part(gather_b.finish, every)},
     )
     gather_b.settle()
     for group in range(2):
@@ -770,7 +772,7 @@
     wait_sent(b_view(0, 15), slots_b.sent)
     pick(
         (0, pairs), crow, mask, books_t, quant, slope, loss,
-        {1: gather_q.step, 3: part(gather_q.back, late), 5: part(gather_q.finish, every)},
+        {0: part(gather_q.finish, every)},
     )
 
     d_dec = feat_real
@@ -813,37 +815,35 @@
         (0, pairs), decode_refs, loss, {1: scatter_b.round_two, 3: scatter_b.round_three}
     )
 
-    grad_out = dot_nt(hidden[...], d_out[...])
-    for k, start, stop in edges:
-        square[k, :, 0 : stop - start] = grad_out[:, start:stop]
-    flatten_out(square, flat)
-    low = enc_rows + dec_rows
-    for j in range(2):
-        near_part = flat[pl.ds(2 * side + j, out_rows, stride=4), :]
-        far_part = flat[pl.ds(2 * other + j, out_rows, stride=4), :]
-        acc_p[low : low + out_rows, cols(j)] = near_part
-        stage_p[low : low + out_rows, cols(j)] = far_part.astype(BF)
+    far_rows = pl.ds(pl.multiple_of(other * half, half), half)
+    near_rows = pl.ds(pl.multiple_of(side * half, half), half)
+    turned = dec_t
+
+    def shifted_grads(values, low, grad):
+        count, span = values.shape[0], turned.shape[1]
+        for k, shift in enumerate((before, None, after)):
+            far, near = 0.0, 0.0
+            for start in range(0, values.shape[1], span):
+                here = slice(start, start + span)
+                left = values.at[:, here]
+                if shift is not None:
+                    left = turned.at[0:count, :]
+                    left[...] = shift(values[:, here])
+                far += dot_nt(left[...], grad[far_rows, here])
+                near += dot_nt(left[...], grad[near_rows, here])
+            rows = slice(low + k * count, low + (k + 1) * count)
+            stage_p[rows, :] = far.astype(BF)
+            acc_p[rows, :] = near
 
     landed, slots = (one_p, two_p, three_p), Slots()
-    scatter_d = Scatter((6, 16), p_rows, acc_p, stage_p, got_p, landed, slots)
+    scatter_d = Scatter((6, 14), p_rows, acc_p, stage_p, got_p, landed, slots)
     scatter_e = Scatter((0, 6), p_rows, acc_p, stage_p, got_p, landed, slots)
-    near_rows = pl.ds(pl.multiple_of(side * half, half), half)
-    far_rows = pl.ds(pl.multiple_of(other * half, half), half)
-    for k, shift in ((1, None), (0, before), (2, after)):
-        values = quant
-        if shift is not None:
-            values = hidden
-            hidden[...] = shift(quant[...])
-        rows = slice(enc_rows + k * width, enc_rows + (k + 1) * width)
-        stage_p[rows, :] = dot_nt(values[...], d_dec[far_rows, :]).astype(BF)
-        if k == 2:
-            scatter_d.pair.start()
-            scatter_b.settle()
-            scatter_b.drain()
-        acc_p[rows, :] = dot_nt(values[...], d_dec[near_rows, :])
-    d_out[...] = before(sig[...])
-    hidden[0:samples, :] = after(sig[...])
-    shifted = (d_out, sig, hidden.at[0:samples, :])
+    scatter_o = Scatter((14, 16), p_rows, acc_p, stage_p, got_p, landed, slots)
+    shifted_grads(quant, enc_rows, d_dec)
+    scatter_d.pair.start()
+    scatter_b.settle()
+    scatter_b.drain()
+
     valid = jnp.sum(mask[...])
     lost = jnp.sum(loss[...])
     first_lane = lax.broadcasted_iota(jnp.int32, (8, 128), 1) == 0
@@ -878,14 +878,20 @@
     zstat[z] = stat[4] + stat[5]
     for k in (1, 2, 3):
         copy_to(level_dev(around(k)), zstat.at[z], zstat.at[z], level_sent, level_got).start()
-    for k, values in enumerate(shifted):
-        rows = slice(k * samples, (k + 1) * samples)
-        stage_p[rows, :] = dot_nt(values[...], slope[far_rows, :]).astype(BF)
+    shifted_grads(sig, 0, slope)
     scatter_e.pair.start()
-    for k, values in enumerate(shifted):
-        rows = slice(k * samples, (k + 1) * samples)
-        acc_p[rows, :] = dot_nt(values[...], slope[near_rows, :])
+    grad_out = dot_nt(hidden[...], d_out[...])
+    for k, start, stop in edges:
+        square[k, :, 0 : stop - start] = grad_out[:, start:stop]
     scatter_e.round_one()
+    flatten_out(square, flat)
+    low = enc_rows + dec_rows
+    for j in range(2):
+        near_part = flat[pl.ds(2 * side + j, out_rows, stride=4), :]
+        far_part = flat[pl.ds(2 * other + j, out_rows, stride=4), :]
+        acc_p[low : low + out_rows, cols(j)] = near_part
+        stage_p[low : low + out_rows, cols(j)] = far_part.astype(BF)
+    scatter_o.pair.start()
     scatter_d.round_three()
     wait_got(zstat.at[0:3], level_got)
     wait_sent(zstat.at[0:3], level_sent)
@@ -894,9 +900,13 @@
     for j in range(2):
         grad_b[pl.ds(j, b_rows, stride=2), :] = acc_b[own_b, cols(j)]
     scatter_e.round_two()
+    scatter_o.round_one()
     scatter_d.settle()
     scatter_e.round_three()
+    scatter_o.round_two()
     scatter_e.settle()
+    scatter_o.round_three()
+    scatter_o.settle()
 
     own_p = pl.ds(pl.multiple_of(spot * p_rows, 16), p_rows)
     swap = copy_to(pair_dev, acc_p.at[own_p, :], last, take("send"), take("recv"))

time: 131 us -> 125 us (0.954)
  Pallas kernels: 130 us -> 124 us
    pallas_call x1, Pallas kernels: 127 us -> 121 us  [fused(): pl.pallas_call(functools.partial(fused_kernel, 3 * samples, 3 * width), o...]
where the time goes in v1:
time: 125 us
  Pallas kernels  124 us (99%)
    pallas_call x1, Pallas kernels, fused(): pl.pallas_call(functools.partial(fused_kernel, 3 * samples, 3 * width), o...  121 us
    pallas_call x1, Pallas kernels, fused(): pl.pallas_call(functools.partial(update_kernel, all_clips, 3 * samples *...  2.81 us

profile of v1, /device:TPU:0, one launch (start us, length us, event | category | flops | bytes accessed | tf_op | source)
XLA Modules:
  0.0 124.6 jit_solution(1808694698513066583)
XLA Ops:
  0.6 121.0 %train_step.1 = (f32[704,128]{1,0:T(8,128)}, f32[256,128]{1,0:T(8,128)}, f32[8,128]{1,0:T(8,128)}) custom-call(bf16[12,320,232]{2,1,0:T(8,128)(2,1)} %bitcast.16, s32[24]{0:T(128)} %lens.1, s32[2,2,24,232]{3,2,1,0:T(8,128)} %codes.1, bf16[960,512]{1,0:T(8,128)(2,1)} %disc.1, f32[1,512]{1,0:T(1,128)} %bitcast.25, bf16[320,320]{1,0:T(8,128)(2,1)} %constant.4.clone.spec, ...), custom_call_target="tpu_custom_call" | custom-call | tf_op jit(solution)/shard_map/train_step/pallas_call | solution.py:943
  121.6 2.8 %train_update.1 = (f32[704,128]{1,0:T(8,128)}, f32[704,128]{1,0:T(8,128)}, f32[704,128]{1,0:T(8,128)}, f32[256,128]{1,0:T(8,128)}, f32[256,128]{1,0:T(8,128)}, /...) custom-call(f32[704,128]{1,0:T(8,128)} %get-tuple-element.19.grad_p, f32[256,128]{1,0:T(8,128)} %get-tuple-element.20.grad_b, ...), custom_call_target="tpu_custom_call" | custom-call | tf_op jit(solution)/shard_map/train_update/pallas_call | solution.py:997

commit v2 on v1

--- a/solution.py
+++ b/solution.py
@@ -40,16 +40,19 @@
     return pl.ds(pl.multiple_of(index * width, width), width)
 
 
-def loop(bounds, step, hooks):
+def loop(bounds, step, hooks, per=1):
     hooks = dict(hooks)
 
     def body(index, carry):
-        step(index)
+        turns = [step(index * per + k) for k in range(per)]
+        turns = [turn for turn in turns if turn is not None]
+        while turns:
+            turns = [turn for turn in turns if next(turn, turns) is not turns]
         for after_index, hook in hooks.items():
-            pl.when(index == after_index)(hook)
+            pl.when(index == after_index // per)(hook)
         return carry
 
-    lax.fori_loop(*bounds, body, 0)
+    lax.fori_loop(bounds[0] // per, bounds[1] // per, body, 0)
 
 
 def col_sum(values):
@@ -126,7 +129,7 @@
         here = lanes(pair, WIDE)
         latent[:, here] = dot(enc_t[...], stack_three(sig[:, here])).astype(BF)
 
-    loop(pairs, step, hooks)
+    loop(pairs, step, hooks, 2)
 
 
 def pick(pairs, crow, mask, books_t, quant, slope, loss, hooks=()):
@@ -149,7 +152,7 @@
             slope[rows, here] = (gap * (-2.0 / width)).astype(BF)
         loss[...] += lost * (1.0 / width)
 
-    loop(pairs, step, hooks)
+    loop(pairs, step, hooks, 2)
 
 
 def book_grad(clip_count, crow, slope, which, rows):
@@ -162,7 +165,7 @@
     return total
 
 
-def decode(pairs, refs, loss, hooks=()):
+def decode(pairs, refs, loss, hooks=(), per=1):
     (quant, dec_t, out, out_t, mask, sig, spec, spec_t, disc, disc_t, score_col) = refs[:11]
     (feat_real, mag_real, hidden, d_out, d_dec) = refs[11:]
     samples = spec.shape[0]
@@ -170,14 +173,16 @@
     half = samples // 2
 
     def step(pair):
-        here = lanes(pair, WIDE)
+        here = lanes(pair, LANES)
         own = mask[:, here]
         pre_dec = dot(dec_t[...], stack_three(quant[:, here]))
         act, act_slope = silu_parts(pre_dec)
         act = act.astype(BF)
+        yield
         hidden[:, here] = act
         tanh_out = jnp.tanh(dot(out_t[...], act))
         made = tanh_out * own
+        yield
         wave_gap = made - sig[:, here].astype(F32)
         norm = wave_gap * wave_gap + 1.0
         root = lax.rsqrt(norm)
@@ -186,6 +191,7 @@
         made_low = made.astype(BF)
 
         spec_fake = dot(spec_t[...], made_low)
+        yield
         real_part, imag_part = spec_fake[:half], spec_fake[half:]
         norm = real_part * real_part + imag_part * imag_part + 1.0
         root = lax.rsqrt(norm)
@@ -195,11 +201,13 @@
         lost += col_sum(norm * gap_root - 1.0) * (1.0 / samples)
         d_mag = spec_gap * gap_root * root * (1.0 / samples)
         d_spec = jnp.concatenate([d_mag * real_part, d_mag * imag_part], axis=0).astype(BF)
+        yield
         d_made += dot(spec[...], d_spec)
 
         pre_fake = dot(disc_t[...], stack_three(made_low))
+        yield
         feat_fake, feat_slope = silu_parts(pre_fake)
-        weight = jnp.concatenate([score_col[...]] * (WIDE // 128), axis=1)
+        weight = jnp.concatenate([score_col[...]] * (LANES // 128), axis=1)
         miss = 1.0 - col_sum(feat_fake * weight)
         feat_gap = feat_fake - feat_real[:, here].astype(F32)
         norm = feat_gap * feat_gap + 1.0
@@ -207,15 +215,18 @@
         lost += own * (miss * miss + col_sum(norm * root - 1.0) * (1.0 / width))
         d_feat = (-2.0 * own * miss) * weight + (own * (1.0 / width)) * (feat_gap * root)
         d_fake = (d_feat * feat_slope).astype(BF)
+        yield
         back = dot(disc[...], d_fake)
         d_made += after(back[:samples]) + back[samples : 2 * samples] + before(back[2 * samples :])
 
+        yield
         d_pre_out = (d_made * own * (1.0 - tanh_out * tanh_out)).astype(BF)
         d_out[:, here] = d_pre_out
         d_dec[:, here] = (dot(out[...], d_pre_out) * act_slope).astype(BF)
-        loss[...] += lost
-
-    loop(pairs, step, hooks)
+        yield
+        loss[:, 0:LANES] += lost
+
+    loop((pairs[0] * 2, pairs[1] * 2), step, hooks, per)
 
 
 def latent_back(pairs, dec, d_dec, mask, slope, d_latent, hooks=()):
@@ -224,11 +235,12 @@
     def step(pair):
         here = lanes(pair, WIDE)
         back = dot(dec[...], d_dec[:, here])
+        yield
         joined = after(back[:width]) + back[width : 2 * width] + before(back[2 * width :])
         joined = joined.astype(BF).astype(F32) * mask[:, here]
         d_latent[:, here] = (joined - slope[:, here].astype(F32)).astype(BF)
 
-    loop(pairs, step, hooks)
+    loop(pairs, step, hooks, 2)
 
 
 def local_kernel(
@@ -387,7 +399,7 @@
 ENC_RATE, DEC_RATE, OUT_RATE, BOOK_RATE = 0.65, 0.14, 0.2, 3.9
 CHIPS = (4, 2, 2)
 SENDS, ARRIVALS = 16, 72
-WAVES = 4
+WAVES = 2
 
 
 def cols(index, width=128):
@@ -812,7 +824,7 @@
         feat_real, mag_real, hidden, d_out, d_dec,
     )
     decode(
-        (0, pairs), decode_refs, loss, {1: scatter_b.round_two, 3: scatter_b.round_three}
+        (0, pairs), decode_refs, loss, {3: scatter_b.round_two, 7: scatter_b.round_three}, 3
     )
 
     far_rows = pl.ds(pl.multiple_of(other * half, half), half)

time: 125 us -> 119 us (0.952)
  Pallas kernels: 124 us -> 117 us
    pallas_call x1, Pallas kernels: 121 us -> 114 us  [fused(): pl.pallas_call(functools.partial(fused_kernel, 3 * samples, 3 * width), o...]
where the time goes in v2:
time: 119 us; the launch traced here: 118 us
  Pallas kernels  117 us (98%)
    pallas_call x1, Pallas kernels, fused(): pl.pallas_call(functools.partial(fused_kernel, 3 * samples, 3 * width), o...  114 us
    pallas_call x1, Pallas kernels, fused(): pl.pallas_call(functools.partial(update_kernel, all_clips, 3 * samples *...  2.81 us

profile of v2, /device:TPU:0, one launch (start us, length us, event | category | flops | bytes accessed | tf_op | source)
XLA Modules:
  0.0 118.0 jit_solution(468831579449991942)
XLA Ops:
  0.6 114.4 %train_step.1 = (f32[704,128]{1,0:T(8,128)}, f32[256,128]{1,0:T(8,128)}, f32[8,128]{1,0:T(8,128)}) custom-call(bf16[12,320,232]{2,1,0:T(8,128)(2,1)} %bitcast.16, s32[24]{0:T(128)} %lens.1, s32[2,2,24,232]{3,2,1,0:T(8,128)} %codes.1, bf16[960,512]{1,0:T(8,128)(2,1)} %disc.1, f32[1,512]{1,0:T(1,128)} %bitcast.25, bf16[320,320]{1,0:T(8,128)(2,1)} %constant.4.clone.spec, ...), custom_call_target="tpu_custom_call" | custom-call | tf_op jit(solution)/shard_map/train_step/pallas_call | solution.py:955
  115.0 2.8 %train_update.1 = (f32[704,128]{1,0:T(8,128)}, f32[704,128]{1,0:T(8,128)}, f32[704,128]{1,0:T(8,128)}, f32[256,128]{1,0:T(8,128)}, f32[256,128]{1,0:T(8,128)}, /...) custom-call(f32[704,128]{1,0:T(8,128)} %get-tuple-element.19.grad_p, f32[256,128]{1,0:T(8,128)} %get-tuple-element.20.grad_b, ...), custom_call_target="tpu_custom_call" | custom-call | tf_op jit(solution)/shard_map/train_update/pallas_call | solution.py:1009
